TPU v7x, 256 devices: a whole 4x4x8 slice. The times are simulated.
256 devices in a mesh: lat: 8 (over y_lo, x), lon: 32 (over z, y_hi, core).
Axes of the slice: x: 4, y: 4 (y_hi: 2, y_lo: 2; y = y_hi * 2 + y_lo), z: 8, core: 2. Of those that a mesh axis runs over, the one named last changes fastest.
Arguments:
- background: bfloat16 [69, 64, 32, 8, 128], P(None, None, 'lon', 'lat'), may hold values from -6 to 6
- obs_ens: bfloat16 [4, 8, 32, 32, 64, 128], P(None, 'lat', 'lon'), may hold values from -6 to 6
- obs_value: bfloat16 [4, 8, 32, 32, 128], P(None, 'lat', 'lon'), may hold values from -10 to 10
- obs_prec: bfloat16 [4, 8, 32, 32, 128], P(None, 'lat', 'lon'), may hold values from 0.019897461 to 0.5
- obs_count: int32 [4, 8, 32], P(None, 'lat', 'lon'), may hold values from 32 to 128, as said below
- slot_owner: int32 [4], replicated, may hold values from 0 to 31
- region_slots: int32 [64, 128, 2], P('lon', 'lat'), may hold values from 0 to 3, as said below
Outputs:
- analysis: bfloat16 [69, 64, 32, 8, 128], P(None, None, 'lon', 'lat')
Inputs may be any that keep to these rules, and one draw needn't show every extreme that they name: The first obs_count entries of a patch's block in a slot are live; the largest value 128 occurs in every draw. `region_slots`: the 2 slots of a region are distinct.
All inputs are finite; a program needn't handle non-finite values.
Results may differ from a plain program's by a relative error of at most 0.0095.
Values may be sent and summed in bfloat16 or wider, within the bound.
No kernel may reach another device: no remote copies, remote signals or barrier semaphores. Data moves between devices by JAX's collectives and lax.ppermute only.
A program may use at most 64 MiB of HBM per device.

v0:
```python
import math

import jax
import jax.numpy as jnp
from jax import lax
from jax.sharding import PartitionSpec as P

CELLS_LAT = 32
CELLS_LON = 4
SLOTS = 4
NEWTON_STEPS = 3


exact_mode = lax.Precision.HIGHEST
TABLE_EXT = (((1, 0.25), (0, 0.75)), ((1, 0.75), (0, 0.25)))


def padded_2(block, sides, width, periodic):
    for axis, dim in sides:
        count = lax.axis_size(axis)
        forward = [(i, i + 1) for i in range(count - 1)]
        if periodic:
            forward.append((count - 1, 0))
        backward = [(target, source) for source, target in forward]
        low = lax.ppermute(
            lax.slice_in_dim(block, block.shape[dim] - width, None, axis=dim), axis, forward
        )
        high = lax.ppermute(lax.slice_in_dim(block, 0, width, axis=dim), axis, backward)
        block = jnp.concatenate([low, block, high], axis=dim)
    return block


def block_gram(ens_block, value_block, prec_block, live_count):
    ens_float = ens_block.astype(jnp.float32)
    obs_mean = jnp.mean(ens_float, axis=0)
    obs_pert = (ens_float - obs_mean[None, :]).astype(jnp.bfloat16)
    position = lax.broadcasted_iota(jnp.int32, value_block.shape, 0)
    weight = jnp.where(position < live_count, prec_block.astype(jnp.float32), 0.0)
    weighted = (obs_pert.astype(jnp.float32) * weight[None, :]).astype(jnp.bfloat16)
    gram_slot = lax.dot_general(
        weighted, obs_pert, (((1,), (1,)), ((), ())), preferred_element_type=jnp.float32
    )
    innovation = value_block.astype(jnp.float32) - obs_mean
    projected = jnp.sum(weighted.astype(jnp.float32) * innovation[None, :], axis=1)
    return (gram_slot, projected)


def region_transform(gram_sum, proj_sum, newton_steps):
    members = gram_sum.shape[-1]
    identity = jnp.eye(members, dtype=jnp.float32)
    matrix = gram_sum + (members - 1.0) * identity
    scaling = jnp.trace(matrix, axis1=-2, axis2=-1) / members
    iterate = matrix / scaling[..., None, None]
    inverse = jnp.broadcast_to(identity, matrix.shape)
    for step_index in range(newton_steps):
        factor = 1.5 * identity - 0.5 * jnp.einsum(
            "...ij,...jk->...ik", inverse, iterate, precision=exact_mode
        )
        iterate = jnp.einsum("...ij,...jk->...ik", iterate, factor, precision=exact_mode)
        inverse = jnp.einsum("...ij,...jk->...ik", factor, inverse, precision=exact_mode)
    root_inv = inverse / jnp.sqrt(scaling)[..., None, None]
    inner_part = jnp.einsum("...ij,...j->...i", root_inv, proj_sum, precision=exact_mode)
    mean_weight = jnp.einsum("...ij,...j->...i", root_inv, inner_part, precision=exact_mode)
    transform = math.sqrt(members - 1.0) * root_inv + mean_weight[..., :, None]
    return transform.astype(jnp.bfloat16)


def interpolate(pert_cells, padded, tapers):
    lon_len = pert_cells.shape[2]
    lat_len = pert_cells.shape[4]
    lon_parts = []
    for lon_par in range(2):
        lat_parts = []
        for lat_par in range(2):
            quarter = pert_cells[:, :, :, lon_par, :, lat_par]
            summed = jnp.zeros(quarter.shape, jnp.float32)
            for lon_off, lon_w in tapers[lon_par]:
                for lat_off, lat_w in tapers[lat_par]:
                    window = padded[lon_off : lon_off + lon_len, lat_off : lat_off + lat_len]
                    product = jnp.einsum(
                        "vklm,lmkj->vjlm", quarter, window, preferred_element_type=jnp.float32
                    )
                    summed = summed + lon_w * lat_w * product
            lat_parts.append(summed)
        lon_parts.append(jnp.stack(lat_parts, axis=-1))
    return jnp.stack(lon_parts, axis=3)


def fold_edges(array_in, along):
    length = array_in.shape[along]
    head_part = lax.slice_in_dim(array_in, 2, 3, axis=along) + lax.slice_in_dim(
        array_in, 0, 1, axis=along
    )
    middle = lax.slice_in_dim(array_in, 3, length - 3, axis=along)
    tail_part = lax.slice_in_dim(array_in, length - 3, length - 2, axis=along) + lax.slice_in_dim(
        array_in, length - 1, length, axis=along
    )
    return jnp.concatenate([head_part, middle, tail_part], axis=along)


def shards(background, obs_ens, obs_value, obs_prec, obs_count, slot_owner, region_slots):
    lon_index = lax.axis_index("lon")
    members = background.shape[1]
    fields = background.shape[0]
    cells_lon = CELLS_LON
    cells_lat = CELLS_LAT
    patch_state = background.reshape(fields, members, cells_lon, cells_lat)
    gram_list = []
    proj_list = []
    for slot_index in range(SLOTS):
        stacked = jnp.concatenate(
            [
                obs_ens[slot_index, 0, 0],
                obs_value[slot_index, 0, 0][:, None, :],
                obs_prec[slot_index, 0, 0][:, None, :],
            ],
            axis=1,
        )
        is_owner = lon_index == slot_owner[slot_index]

        def owner_term(start, count, stacked=stacked, is_owner=is_owner):
            rows = stacked.astype(jnp.float32)
            return jnp.where(is_owner, rows, 0.0)

        received = lax.psum_scatter(
            owner_term(jnp.int32(0), lax.axis_size("lon") * 1).astype(jnp.bfloat16),
            "lon",
            scatter_dimension=0,
            tiled=True,
        )
        own_ens = received[0, :members]
        own_value = received[0, members]
        own_prec = received[0, members + 1]
        gram_slot, projected = block_gram(own_ens, own_value, own_prec, obs_count[slot_index, 0, 0])
        gram_list.append(gram_slot)
        proj_list.append(projected)
    lon_pairs = region_slots.shape[0]
    lat_pairs = region_slots.shape[1]
    gram_sum = jnp.zeros((lon_pairs, lat_pairs, members, members), jnp.float32)
    proj_sum = jnp.zeros((lon_pairs, lat_pairs, members), jnp.float32)
    for slot_index in range(SLOTS):
        member = jnp.sum((region_slots == slot_index).astype(jnp.float32), axis=-1)
        gram_sum = gram_sum + member[:, :, None, None] * gram_list[slot_index]
        proj_sum = proj_sum + member[:, :, None] * proj_list[slot_index]
    transforms = region_transform(gram_sum, proj_sum, NEWTON_STEPS)
    back_float = patch_state.astype(jnp.float32)
    back_mean = jnp.mean(back_float, axis=1, keepdims=True)
    pert = (back_float - back_mean).astype(jnp.bfloat16)
    lon_extended = padded_2(pert, (("lon", 2),), 1, True)
    extended = padded_2(lon_extended, (("lat", 3),), 1, False)
    local_padded = jnp.pad(transforms, ((1, 1), (1, 1), (0, 0), (0, 0)))
    ext_cells = extended.reshape(fields, members, lon_pairs + 1, 2, lat_pairs + 1, 2)
    partial_value = interpolate(ext_cells, local_padded, TABLE_EXT).reshape(
        fields, members, cells_lon + 2, cells_lat + 2
    )
    lon_summed = padded_2(partial_value, (("lon", 2),), 1, True)
    folded = fold_edges(lon_summed, 2)
    lat_summed = padded_2(folded, (("lat", 3),), 1, False)
    increment = fold_edges(lat_summed, 3)
    result = (back_mean + increment).astype(jnp.bfloat16)
    return result.reshape(fields, members, 1, 1, cells_lon * cells_lat)


def solution(mesh):
    in_specs = (
        P(None, None, "lon", "lat", None),
        P(None, "lat", "lon", None, None, None),
        P(None, "lat", "lon", None, None),
        P(None, "lat", "lon", None, None),
        P(None, "lat", "lon"),
        P(),
        P("lon", "lat", None),
    )
    out_specs = P(None, None, "lon", "lat", None)
    return jax.shard_map(shards, mesh=mesh, in_specs=in_specs, out_specs=out_specs, check_vma=False)
```

profile of v0, /device:TPU:6, one launch (start us, length us, event | category | flops | bytes accessed | tf_op | source)
XLA Modules:
  0.0 412.5 jit_solution(6587083624553575581)
XLA Ops:
  6.5 1.5 fusion.100
  12.2 1.7 slice_bitcast_fusion.23
  14.0 1.4 select_convert_fusion.2
  15.3 1.3 select_convert_fusion
  17.9 1.9 copy.90
  21.2 2.2 subtract_convert_fusion
  23.6 8.0 %collective-permute-start.1 = (bf16[69,64,1,32]{0,3,2,1:T(8,128)(2,1)S(1)}, bf16[69,64,1,32]{0,3,2,1:T(8,128)(2,1)S(1)}, u32[]{:S(2)}, u32[]{:S(2)}) collective-permute-start(bf16[69,64,1,32]{0,3,2,1:T(8,128)(2,1)S(1)} %get-tuple-element.20), channel_id=1, source_target_pairs={{1,0},{2,1},{3,2},{4,3},{5,4},{6,5},{7,6},{8,7},{9,8},{10,9},{11,1... | collective-permute-start | bytes 847880 | tf_op jit(solution)/shard_map/ppermute | solution.py:28
  32.3 7.0 %collective-permute-done = bf16[69,64,1,32]{0,3,2,1:T(8,128)(2,1)S(1)} collective-permute-done((bf16[69,64,1,32]{0,3,2,1:T(8,128)(2,1)S(1)}, bf16[69,64,1,32]{0,3,2,1:T(8,128)(2,1)S(1)}, u32[]{:S(2)}, u32[]{:S(2)}) %collective-permute-start) | collective-permute-done | bytes 282656 | tf_op jit(solution)/shard_map/ppermute | solution.py:25
  40.4 2.1 collective-permute-start.2
  42.6 3.7 collective-permute-start.3
  46.9 1.4 collective-permute-done.2
  48.3 4.4 %collective-permute-done.3 = bf16[69,64,6,1]{0,3,2,1:T(2,128)(2,1)} collective-permute-done((bf16[69,64,6,1]{0,3,2,1:T(2,128)(2,1)S(1)}, bf16[69,64,6,1]{0,3,2,1:T(2,128)(2,1)}, u32[]{:S(2)}, u32[]{:S(2)}) %collective-permute-start.3) | collective-permute-done | bytes 53024 | tf_op jit(solution)/shard_map/ppermute | solution.py:28
  52.7 4.0 pad_maximum_fusion.3
  57.6 240.7 %all-reduce.8.cloned.1.call-done = (bf16[32,66,128]{2,1,0:T(8,128)(2,1)}, bf16[32,66,128]{2,1,0:T(8,128)(2,1)}, bf16[32,66,128]{2,1,0:T(8,128)(2,1)}, bf16[32,66,128]{2,1,0:T(8,128)(2,1)}) async-done(((bf16[32,66,128]{2,1,0:T(8,128)(2,1)}, bf16[32,66,128]{2,1,0:T(8,128)(2,1)}, bf16[32,66,128]{2,1,0:T(8,128)(2,1)}, bf16[32,66,128]{2,1,0:T(8,128)(2,1)}), (bf16[32,66,128]{2,1,0:T(8,128)(2,1)}, ...) | async-done | bytes 2162704
  298.3 1.3 convert_reduce_fusion.1
  299.6 1.3 convert_reduce_fusion.2
  300.9 1.3 convert_reduce_fusion.3
  302.2 1.3 convert_reduce_fusion.4
  303.5 2.0 fusion.79
  305.5 1.5 fusion.38
  307.0 2.0 fusion.82
  308.9 1.5 fusion.41
  310.4 2.0 fusion.85
  312.4 1.9 fusion.88
  314.2 1.5 fusion.44
  315.7 1.5 fusion.47
  317.8 1.4 fusion.2
  319.3 1.6 fusion.16
  325.6 1.4 multiply_reduce_fusion.3
  327.0 1.4 multiply_reduce_fusion.2
  328.4 1.4 multiply_reduce_fusion.1
  329.8 1.4 multiply_reduce_fusion
  331.2 1.2 fusion
  332.4 1.4 convolution_divide_fusion
  333.9 1.7 convolution_bitcast_fusion
  335.6 1.7 fusion.103
  346.1 1.5 pad_maximum_fusion
  347.5 1.4 copy.120
  349.2 18.6 %collective-permute-done.4 = f32[69,64,1,34]{0,1,3,2:T(8,128)S(1)} collective-permute-done((f32[69,64,1,34]{0,1,3,2:T(8,128)S(1)}, f32[69,64,1,34]{0,1,3,2:T(8,128)S(1)}, u32[]{:S(2)}, u32[]{:S(2)}) %collective-permute-start.4) | collective-permute-done | bytes 600608 | tf_op jit(solution)/shard_map/ppermute | solution.py:25
  368.3 12.9 %collective-permute-done.5 = f32[69,64,1,34]{0,1,3,2:T(8,128)S(1)} collective-permute-done((f32[69,64,1,34]{0,1,3,2:T(8,128)S(1)}, f32[69,64,1,34]{0,1,3,2:T(8,128)S(1)}, u32[]{:S(2)}, u32[]{:S(2)}) %collective-permute-start.5) | collective-permute-done | bytes 600608 | tf_op jit(solution)/shard_map/ppermute | solution.py:28
  381.3 2.2 collective-permute-start.6
  383.6 4.6 %collective-permute-done.6 = f32[69,64,4,1]{0,1,3,2:T(8,128)S(1)} collective-permute-done((f32[69,64,4,1]{0,1,3,2:T(8,128)S(1)}, f32[69,64,4,1]{0,1,3,2:T(8,128)S(1)}, u32[]{:S(2)}, u32[]{:S(2)}) %collective-permute-start.6) | collective-permute-done | bytes 70688 | tf_op jit(solution)/shard_map/ppermute | solution.py:25
  388.2 2.8 collective-permute-start.7
  391.9 2.0 copy-done.1
  394.0 3.2 collective-permute-done.7
  397.2 2.1 slice-done
  399.9 2.4 copy.121
  402.8 2.6 copy.122
  (75 shorter events, 24.5 us)
Async XLA Ops:
  6.5 291.8 %all-reduce.8.cloned.1.call-start = ((), (), s32[]{:S(2)}) async-start(), calls=%async_computation | async-start | bytes 4718592
  16.7 1.3 copy-start.2
  19.9 1.4 copy-start
  23.4 8.2 %copy-start.4 = (s32[2,16,2]{1,2,0:T(2,128)S(1)}, s32[2,16,2]{1,2,0:T(2,128)}, u32[]{:S(2)}) copy-start(s32[2,16,2]{1,2,0:T(2,128)} %param.13) | copy-start | bytes 772
  23.4 8.2 %copy-start.3 = (s32[4,1,1]{0,2,1:T(1,128)S(1)}, s32[4,1,1]{0,2,1:T(1,128)}, u32[]{:S(2)}) copy-start(s32[4,1,1]{0,2,1:T(1,128)} %param.11) | copy-start | bytes 52
  23.5 15.8 %collective-permute-start = (bf16[69,64,1,32]{0,3,2,1:T(8,128)(2,1)S(1)}, bf16[69,64,1,32]{0,3,2,1:T(8,128)(2,1)S(1)}, u32[]{:S(2)}, u32[]{:S(2)}) collective-permute-start(bf16[69,64,1,32]{0,3,2,1:T(8,128)(2,1)S(1)} %get-tuple-element.19), channel_id=1, source_target_pairs={{0,1},{1,2},{2,3},{3,4},{4,5},{5,6},{6,7},{7,8},{8,9},{9,10},{10,1... | collective-permute-start | bytes 847880 | tf_op jit(solution)/shard_map/ppermute | solution.py:25
  23.6 15.7 %collective-permute-start.1 = (bf16[69,64,1,32]{0,3,2,1:T(8,128)(2,1)S(1)}, bf16[69,64,1,32]{0,3,2,1:T(8,128)(2,1)S(1)}, u32[]{:S(2)}, u32[]{:S(2)}) collective-permute-start(bf16[69,64,1,32]{0,3,2,1:T(8,128)(2,1)S(1)} %get-tuple-element.20), channel_id=1, source_target_pairs={{1,0},{2,1},{3,2},{4,3},{5,4},{6,5},{7,6},{8,7},{9,8},{10,9},{11,1... | collective-permute-start | bytes 847880 | tf_op jit(solution)/shard_map/ppermute | solution.py:28
  32.3 14.0 %copy-start.5 = (u32[256]{0:T(256)S(1)}, u32[256]{0:T(256)}, u32[]{:S(2)}) copy-start(u32[256]{0:T(256)} %constant.57) | copy-start | bytes 3076
  40.4 7.9 %collective-permute-start.2 = (bf16[69,64,6,1]{0,3,2,1:T(2,128)(2,1)}, bf16[69,64,6,1]{0,3,2,1:T(2,128)(2,1)}, u32[]{:S(2)}, u32[]{:S(2)}) collective-permute-start(bf16[69,64,6,1]{0,3,2,1:T(2,128)(2,1)} %get-tuple-element.17), channel_id=1, source_target_pairs={{0,32},{32,64},{64,96},{96,128},{128,160},{160,192},{192,224},{1,3... | collective-permute-start | bytes 158984 | tf_op jit(solution)/shard_map/ppermute | solution.py:25
  42.6 10.1 %collective-permute-start.3 = (bf16[69,64,6,1]{0,3,2,1:T(2,128)(2,1)S(1)}, bf16[69,64,6,1]{0,3,2,1:T(2,128)(2,1)}, u32[]{:S(2)}, u32[]{:S(2)}) collective-permute-start(bf16[69,64,6,1]{0,3,2,1:T(2,128)(2,1)S(1)} %get-tuple-element.18), channel_id=1, source_target_pairs={{32,0},{64,32},{96,64},{128,96},{160,128},{192,160},{224,192},{33,... | collective-permute-start | bytes 158984 | tf_op jit(solution)/shard_map/ppermute | solution.py:28
  349.1 18.7 %collective-permute-start.4 = (f32[69,64,1,34]{0,1,3,2:T(8,128)S(1)}, f32[69,64,1,34]{0,1,3,2:T(8,128)S(1)}, u32[]{:S(2)}, u32[]{:S(2)}) collective-permute-start(f32[69,64,1,34]{0,1,3,2:T(8,128)S(1)} %slice.235), channel_id=1, source_target_pairs={{0,1},{1,2},{2,3},{3,4},{4,5},{5,6},{6,7},{7,8},{8,9},{9,10},{10,1... | collective-permute-start | bytes 1801736 | tf_op jit(solution)/shard_map/ppermute | solution.py:25
  368.1 13.1 %collective-permute-start.5 = (f32[69,64,1,34]{0,1,3,2:T(8,128)S(1)}, f32[69,64,1,34]{0,1,3,2:T(8,128)S(1)}, u32[]{:S(2)}, u32[]{:S(2)}) collective-permute-start(f32[69,64,1,34]{0,1,3,2:T(8,128)S(1)} %get-tuple-element.14), channel_id=1, source_target_pairs={{1,0},{2,1},{3,2},{4,3},{5,4},{6,5},{7,6},{8,7},{9,8},{10,9},{11,1... | collective-permute-start | bytes 1801736 | tf_op jit(solution)/shard_map/ppermute | solution.py:28
  381.3 6.9 %collective-permute-start.6 = (f32[69,64,4,1]{0,1,3,2:T(8,128)S(1)}, f32[69,64,4,1]{0,1,3,2:T(8,128)S(1)}, u32[]{:S(2)}, u32[]{:S(2)}) collective-permute-start(f32[69,64,4,1]{0,1,3,2:T(8,128)S(1)} %pad_maximum_fusion.8), channel_id=1, source_target_pairs={{0,32},{32,64},{64,96},{96,128},{128,160},{160,192},{192,224},{1,3... | collective-permute-start | bytes 211976 | tf_op jit(solution)/shard_map/ppermute | solution.py:25
  388.2 9.0 %collective-permute-start.7 = (f32[69,64,4,1]{0,1,3,2:T(8,128)S(1)}, f32[69,64,4,1]{0,1,3,2:T(8,128)S(1)}, u32[]{:S(2)}, u32[]{:S(2)}) collective-permute-start(f32[69,64,4,1]{0,1,3,2:T(8,128)S(1)} %get-tuple-element.16), channel_id=1, source_target_pairs={{32,0},{64,32},{96,64},{128,96},{160,128},{192,160},{224,192},{33,... | collective-permute-start | bytes 211976 | tf_op jit(solution)/shard_map/ppermute | solution.py:28
  391.9 2.0 copy-start.1
  397.2 2.1 slice-start
Sparse Core Ops, SparseCore 0:
  16.8 281.4 all-reduce.7
where the time goes:
time: 420 us; the launch traced here: 412 us
  waiting for transfers between devices  293 us (70%)
  other arithmetic  34.8 us (8%)
  matrix products  27.2 us (6%)
  local copies, waits for them, and re-layouts  21.9 us (5%)
  starting transfers between devices  19.1 us (5%)
  between operations  16.7 us (4%)
    unnamed x2, waiting for transfers between devices  241 us
    ppermute x4, waiting for transfers between devices, padded_2(): lax.ppermute(lax.slice_in_dim(block, block.shape[dim] - width, None, axis...  31.6 us
    ppermute x4, waiting for transfers between devices, padded_2(): lax.ppermute(lax.slice_in_dim(block, 0, width, axis=dim), axis, backward)  20.5 us
    ppermute x4, starting transfers between devices, padded_2(): lax.ppermute(lax.slice_in_dim(block, 0, width, axis=dim), axis, backward)  14.6 us
  transfers between devices with their start and end apart: 9, of which 8 were waited for; matrix products, arithmetic and copies ran while one was open for 3% of the time, Pallas kernels for 0%

commit v1 on v0

v1 whole, which is shorter than its diff:
```python
import math

import jax
import jax.numpy as jnp
import numpy as np
from jax import lax
from jax.experimental import pallas as pl
from jax.experimental.pallas import tpu as pltpu
from jax.sharding import PartitionSpec as P

MEMBERS = 64
FIELDS = 69
CELLS_LAT = 32
CELLS_LON = 4
PATCH_CELLS = 128
SLOTS = 4
OBS_BLOCK = 128
NEWTON_STEPS = 3
LON_PAIRS = 2
LAT_PAIRS = 16
PAIRS = ((0, 1), (0, 2), (0, 3), (1, 2), (1, 3), (2, 3))
BITS = (0, 1, 2, 3, 4)
ROWS = 66
PAIR_ROWS = 192
EDGE_ROWS = 64
COEF_ROWS = 16
MSG_ROWS = PAIR_ROWS + 2 * EDGE_ROWS + COEF_ROWS


def lon_weight(column, region):
    if column // 2 == region:
        return 0.75
    outer = column // 2 + (1 if column % 2 else -1)
    return 0.25 if outer == region else 0.0


def lat_weight(row, region):
    if row // 2 == region:
        return 0.75
    outer = row // 2 + (1 if row % 2 else -1)
    return 0.25 if outer == region else 0.0


def taper_tables():
    table = np.zeros((LON_PAIRS * LAT_PAIRS, 2 * PATCH_CELLS), np.float32)
    for a in range(LON_PAIRS):
        for b in range(LAT_PAIRS):
            for col in range(CELLS_LON):
                for row in range(CELLS_LAT):
                    cell = col * CELLS_LAT + row
                    lat_w = lat_weight(row, b)
                    table[a * LAT_PAIRS + b, cell] = lon_weight(col, a) * lat_w
                    if col == 0:
                        lon_w = lon_weight(col, a - LON_PAIRS)
                    elif col == CELLS_LON - 1:
                        lon_w = lon_weight(col, a + LON_PAIRS)
                    else:
                        lon_w = 0.0
                    table[a * LAT_PAIRS + b, PATCH_CELLS + cell] = lon_w * lat_w
    sides = np.zeros((2, 2, 3, COEF_ROWS, PATCH_CELLS), np.float32)
    for lat_par in range(2):
        for which in range(2):
            upper = (which == 0) == (lat_par == 0)
            row = CELLS_LAT - 1 if upper else 0
            for lon_par in range(2):
                for source in range(3):
                    if source == 0:
                        shift = 0
                    else:
                        right = (source == 1) == (lon_par == 0)
                        shift = LON_PAIRS if right else -LON_PAIRS
                    for a in range(LON_PAIRS):
                        for col in range(CELLS_LON):
                            sides[lat_par, lon_par, source, 6 + 2 * which + a, col * CELLS_LAT + row] = (
                                0.25 * lon_weight(col, a + shift)
                            )
    masks = np.zeros((2, 2, COEF_ROWS, PATCH_CELLS), np.float32)
    for lon_par in range(2):
        for source in range(2):
            right = (source == 0) == (lon_par == 0)
            first = (CELLS_LON - 1) * CELLS_LAT if right else 0
            masks[lon_par, source, :6, first : first + CELLS_LAT] = 1.0
    return table, sides, masks


TABLE, SIDES, MASKS = taper_tables()


def mm(left, right):
    return lax.dot_general(
        left,
        right,
        (((1,), (0,)), ((), ())),
        precision=lax.Precision.HIGHEST,
        preferred_element_type=jnp.float32,
    )


def transform_kernel(count_ref, edge_ref, block_ref, pair_ref, edges_ref, held_ref):
    f32 = jnp.float32
    members = MEMBERS
    row_id = lax.broadcasted_iota(jnp.int32, (members, members), 0)
    col_id = lax.broadcasted_iota(jnp.int32, (members, members), 1)
    identity = jnp.where(row_id == col_id, 1.0, 0.0).astype(f32)
    position = lax.broadcasted_iota(jnp.int32, (1, OBS_BLOCK), 1)
    grams = []
    projs = []
    for slot in range(SLOTS):
        block = block_ref[slot].astype(f32)
        ens = block[:members]
        value = block[members : members + 1]
        prec = block[members + 1 : members + 2]
        obs_mean = jnp.sum(ens, axis=0, keepdims=True) * (1.0 / members)
        pert = (ens - obs_mean).astype(jnp.bfloat16)
        weight = jnp.where(position < count_ref[slot], prec, 0.0)
        weighted = (pert.astype(f32) * weight).astype(jnp.bfloat16)
        grams.append(
            lax.dot_general(
                weighted, pert, (((1,), (1,)), ((), ())), preferred_element_type=f32
            )
        )
        innovation = value - obs_mean
        projs.append(jnp.sum(weighted.astype(f32) * innovation, axis=1, keepdims=True))
    inverses = []
    iterates = []
    scalings = []
    for first, second in PAIRS:
        matrix = grams[first] + grams[second] + (members - 1.0) * identity
        trace = jnp.sum(jnp.sum(matrix * identity, axis=1, keepdims=True), axis=0, keepdims=True)
        scaling = trace * (1.0 / members)
        scalings.append(scaling)
        iterate = matrix / scaling
        inverses.append(1.5 * identity - 0.5 * iterate)
        iterates.append(iterate)
    iterates = [mm(x, y) for x, y in zip(iterates, inverses)]
    for step in range(1, NEWTON_STEPS):
        factors = [1.5 * identity - 0.5 * mm(y, x) for x, y in zip(iterates, inverses)]
        if step < NEWTON_STEPS - 1:
            iterates = [mm(x, f) for x, f in zip(iterates, factors)]
        inverses = [mm(f, y) for f, y in zip(factors, inverses)]
    roots = [y / jnp.sqrt(s) for y, s in zip(inverses, scalings)]
    sums = [projs[first] + projs[second] for first, second in PAIRS]
    inner = [mm(r, jnp.broadcast_to(p, (members, members))) for r, p in zip(roots, sums)]
    means = [mm(r, p) for r, p in zip(roots, inner)]
    for pair in range(len(PAIRS)):
        transform = math.sqrt(members - 1.0) * roots[pair] + means[pair]
        turned = transform.T
        held_ref[pair] = turned
        half = pair % 2
        pair_ref[pair // 2, :, half * members : (half + 1) * members] = turned.astype(jnp.bfloat16)
    for which in range(2):
        for a in range(LON_PAIRS):
            chosen = held_ref[edge_ref[2 * which + a]]
            edges_ref[which, :, a * members : (a + 1) * members] = chosen.astype(jnp.bfloat16)


def transforms_of(counts, edge_ids, blocks):
    smem = pl.BlockSpec(memory_space=pltpu.SMEM)
    vmem = pl.BlockSpec(memory_space=pltpu.VMEM)
    return pl.pallas_call(
        transform_kernel,
        out_shape=(
            jax.ShapeDtypeStruct((3, MEMBERS, 2 * MEMBERS), jnp.bfloat16),
            jax.ShapeDtypeStruct((2, MEMBERS, 2 * MEMBERS), jnp.bfloat16),
        ),
        in_specs=[smem, smem, vmem],
        out_specs=(vmem, vmem),
        scratch_shapes=[pltpu.VMEM((len(PAIRS), MEMBERS, MEMBERS), jnp.float32)],
        compiler_params=pltpu.CompilerParams(vmem_limit_bytes=16 * 1024 * 1024),
        name="transforms",
    )(counts, edge_ids, blocks)


def analysis_kernel(own_ref, side_ref, other_ref, coef_ref, mask_ref, back_ref, out_ref, left_ref, weight_ref):
    f32 = jnp.float32
    bf16 = jnp.bfloat16
    tiles = (MSG_ROWS - COEF_ROWS) // MEMBERS
    coef_rows = MSG_ROWS - COEF_ROWS
    for source, ref in enumerate((own_ref, side_ref, other_ref)):
        for tile in range(tiles):
            at = (source * tiles + tile) * 2 * MEMBERS
            left_ref[:, at : at + 2 * MEMBERS] = ref[tile * MEMBERS : (tile + 1) * MEMBERS, :]
        if source == 0:
            weight_ref[source] = coef_ref[source].astype(f32)
        else:
            weight_ref[source] = coef_ref[source].astype(f32) + ref[coef_rows:, :].astype(f32) * mask_ref[
                source - 1
            ].astype(f32)

    def fields(first, count):
        perts = []
        means = []
        for f in range(count):
            state = back_ref[first + f].astype(f32)
            mean = jnp.sum(state, axis=0, keepdims=True) * (1.0 / MEMBERS)
            means.append(mean)
            perts.append((state - mean).astype(bf16))
        parts = []
        for source in range(3):
            for k in range(2 * tiles):
                weight = weight_ref[source, k : k + 1, :].astype(bf16)
                parts.append(jnp.concatenate([p * weight for p in perts], axis=1))
        right = jnp.concatenate(parts, axis=0)
        total = lax.dot_general(
            left_ref[...], right, (((1,), (0,)), ((), ())), preferred_element_type=f32
        )
        for f in range(count):
            piece = total[:, f * PATCH_CELLS : (f + 1) * PATCH_CELLS]
            out_ref[first + f] = (piece + means[f]).astype(bf16)

    def step(index, carry):
        fields(index * 2, 2)
        return carry

    lax.fori_loop(0, FIELDS // 2, step, 0)
    if FIELDS % 2:
        fields(FIELDS - 1, 1)


def analysis_of(own, side, other, coefs, masks, background):
    vmem = pl.BlockSpec(memory_space=pltpu.VMEM)
    depth = 3 * (MSG_ROWS - COEF_ROWS) // MEMBERS * 2 * MEMBERS
    return pl.pallas_call(
        analysis_kernel,
        out_shape=jax.ShapeDtypeStruct((FIELDS, MEMBERS, PATCH_CELLS), jnp.bfloat16),
        in_specs=[vmem] * 6,
        out_specs=vmem,
        scratch_shapes=[
            pltpu.VMEM((MEMBERS, depth), jnp.bfloat16),
            pltpu.VMEM((3, COEF_ROWS, PATCH_CELLS), jnp.float32),
        ],
        compiler_params=pltpu.CompilerParams(vmem_limit_bytes=32 * 1024 * 1024),
        name="analysis",
    )(own, side, other, coefs, masks, background)


def scatter_blocks(obs_ens, obs_value, obs_prec, slot_owner, lon_index):
    small = jnp.stack([obs_value[:, 0, 0], obs_prec[:, 0, 0]], axis=2)
    blocks = jnp.concatenate([obs_ens[:, 0, 0], small], axis=2)
    blocks = blocks.reshape((SLOTS, 2, 2, 2, 2, 2, ROWS, OBS_BLOCK))
    axes = {0: 5, 1: 4, 2: 3, 3: 2, 4: 1}
    for bit in BITS:
        axis = axes[bit]
        mine = (lon_index >> bit) & 1
        keep = lax.dynamic_index_in_dim(blocks, mine, axis, keepdims=False)
        send = lax.dynamic_index_in_dim(blocks, 1 - mine, axis, keepdims=False)
        got = lax.ppermute(send, "lon", [(i, i ^ (1 << bit)) for i in range(32)])
        held = ((slot_owner >> bit) & 1) == mine
        blocks = jnp.where(held.reshape((SLOTS,) + (1,) * (keep.ndim - 1)), keep, got)
        axes = {b: (d - 1 if d > axis else d) for b, d in axes.items()}
    return blocks.reshape(SLOTS, ROWS, OBS_BLOCK)


def shards(background, obs_ens, obs_value, obs_prec, obs_count, slot_owner, region_slots):
    lon_index = lax.axis_index("lon")
    lat_index = lax.axis_index("lat")
    lon_par = lon_index & 1
    lat_par = lat_index & 1

    low = jnp.min(region_slots, axis=-1)
    high = jnp.max(region_slots, axis=-1)
    ids = ((low * (7 - low)) >> 1) + (high - low - 1)
    edge_top = ids[:, 0]
    edge_bottom = ids[:, LAT_PAIRS - 1]
    even = lat_par == 0
    edge_ids = jnp.concatenate(
        [jnp.where(even, edge_bottom, edge_top), jnp.where(even, edge_top, edge_bottom)]
    )
    one_hot = (
        lax.broadcasted_iota(jnp.int32, (COEF_ROWS, LON_PAIRS * LAT_PAIRS), 0) == ids.reshape(1, -1)
    ).astype(jnp.bfloat16)
    tapers = lax.dot_general(
        one_hot,
        jnp.asarray(TABLE, jnp.bfloat16),
        (((1,), (0,)), ((), ())),
        preferred_element_type=jnp.float32,
    ).astype(jnp.bfloat16)
    own_taper = tapers[:, :PATCH_CELLS]
    next_taper = tapers[:, PATCH_CELLS:]
    sides = jnp.asarray(SIDES, jnp.bfloat16)[lat_par, lon_par]
    coefs = jnp.concatenate([(sides[0] + own_taper)[None], sides[1:]], axis=0)
    masks = jnp.asarray(MASKS, jnp.bfloat16)[lon_par]

    blocks = scatter_blocks(obs_ens, obs_value, obs_prec, slot_owner, lon_index)
    pair_tiles, edges = transforms_of(obs_count[:, 0, 0], edge_ids, blocks)

    pairs_a = [(i, i ^ 1) for i in range(8)]
    pairs_b = [(i, i + 1) for i in range(1, 7, 2)] + [(i + 1, i) for i in range(1, 7, 2)]
    lat_a = lax.ppermute(edges[0], "lat", pairs_a)
    lat_b = lax.ppermute(edges[1], "lat", pairs_b)
    message = jnp.concatenate(
        [pair_tiles.reshape(PAIR_ROWS, 2 * MEMBERS), lat_a, lat_b, next_taper], axis=0
    )
    swap = [(i, (i + 1) % 32) for i in range(1, 32, 2)] + [((i + 1) % 32, i) for i in range(1, 32, 2)]
    from_core = lax.ppermute(message, "lon", [(i, i ^ 1) for i in range(32)])
    from_next = lax.ppermute(message, "lon", swap)
    state = background.reshape(FIELDS, MEMBERS, PATCH_CELLS)
    result = analysis_of(message, from_core, from_next, coefs, masks, state)
    return result.reshape(FIELDS, MEMBERS, 1, 1, PATCH_CELLS)


def solution(mesh):
    in_specs = (
        P(None, None, "lon", "lat", None),
        P(None, "lat", "lon", None, None, None),
        P(None, "lat", "lon", None, None),
        P(None, "lat", "lon", None, None),
        P(None, "lat", "lon"),
        P(),
        P("lon", "lat", None),
    )
    out_specs = P(None, None, "lon", "lat", None)
    return jax.shard_map(shards, mesh=mesh, in_specs=in_specs, out_specs=out_specs, check_vma=False)
```

time: 420 us -> 88.1 us (0.21); the launches traced: 412 us -> 87.7 us
  waiting for transfers between devices: 293 us -> 32.6 us
  other arithmetic: 34.8 us -> 5.72 us
  matrix products: 27.2 us -> 0.12 us
  between operations: 16.7 us -> 0.24 us
  local copies, waits for them, and re-layouts: 21.9 us -> 6.42 us
  Pallas kernels: 0 us -> 14.7 us
  starting transfers between devices: 19.1 us -> 28 us
    unnamed x2 -> x0, waiting for transfers between devices: 241 us -> none
    dot_general x30 -> x1, matrix products: 27.2 us -> 0.12 us  [shards(): lax.dot_general(one_hot, jnp.asarray(TABLE, jnp.bfloat16), (((1,), (0,)),...]
    ppermute x8 -> x9, waiting for transfers between devices: 52.1 us -> 32.6 us  [the longest x5 26.8 us: scatter_blocks(): got = lax.ppermute(send, 'lon', [(i, i ^ 1 << bit) for i in range(32)])]
    pallas_call x0 -> x2, Pallas kernels: none -> 14.7 us  [the longest x1 12.2 us: analysis_of(): pl.pallas_call(analysis_kernel, out_shape=jax.ShapeDtypeStruct((FIELDS, M...]
    reduce_sum x11 -> x0, other arithmetic: 11.8 us -> none  [the longest x4 5.55 us: block_gram(): jnp.sum(weighted.astype(jnp.float32) * innovation[None, :], axis=1)]
    ppermute x8 -> x9, starting transfers between devices: 19.1 us -> 28 us  [the longest x5 15.2 us: scatter_blocks(): got = lax.ppermute(send, 'lon', [(i, i ^ 1 << bit) for i in range(32)])]
    sub x4 -> x0, other arithmetic: 7.76 us -> none  [block_gram(): innovation = value_block.astype(jnp.float32) - obs_mean]
    unnamed x14 -> x12, local copies, waits for them, and re-layouts: 6.67 us -> 0.03 us
  transfers between devices with their start and end apart: 9 -> 9, of which waited for: 8 -> 7; matrix products, arithmetic and copies ran while one was open for 3% -> 2% of each run, Pallas kernels for 0% -> 0%
where the time goes in v1:
time: 88.1 us; the launch traced here: 87.7 us
  waiting for transfers between devices  32.6 us (37%)
  starting transfers between devices  28 us (32%)
  Pallas kernels  14.7 us (17%)
  local copies, waits for them, and re-layouts  6.42 us (7%)
  other arithmetic  5.72 us (6%)
    ppermute x5, waiting for transfers between devices, scatter_blocks(): got = lax.ppermute(send, 'lon', [(i, i ^ 1 << bit) for i in range(32)])  26.8 us
    ppermute x5, starting transfers between devices, scatter_blocks(): got = lax.ppermute(send, 'lon', [(i, i ^ 1 << bit) for i in range(32)])  15.2 us
    pallas_call x1, Pallas kernels, analysis_of(): pl.pallas_call(analysis_kernel, out_shape=jax.ShapeDtypeStruct((FIELDS, M...  12.2 us
    ppermute x1, starting transfers between devices, shards(): from_next = lax.ppermute(message, 'lon', swap)  7.69 us
    ppermute x1, starting transfers between devices, shards(): lat_b = lax.ppermute(edges[1], 'lat', pairs_b)  4.05 us
    ppermute x1, waiting for transfers between devices, shards(): lat_b = lax.ppermute(edges[1], 'lat', pairs_b)  3.65 us
    select_n x5, other arithmetic, scatter_blocks(): jnp.where(held.reshape((SLOTS,) + (1,) * (keep.ndim - 1)), keep, got)  2.66 us
    pallas_call x1, Pallas kernels, transforms_of(): pl.pallas_call(transform_kernel, out_shape=(jax.ShapeDtypeStruct((3, MEMB...  2.54 us
  transfers between devices with their start and end apart: 9, of which 7 were waited for; matrix products, arithmetic and copies ran while one was open for 2% of the time, Pallas kernels for 0%

profile of v1, /device:TPU:6, one launch (start us, length us, event | category | flops | bytes accessed | tf_op | source)
XLA Modules:
  0.0 87.7 jit_solution(14869456940993254282)
XLA Ops:
  0.0 0.8 copy.37
  0.8 0.8 copy.38
  1.6 2.1 %pad_maximum_fusion = bf16[4,2,2,2,2,2,66,128]{7,6,5,4,3,2,1,0:T(8,128)(2,1)S(1)} fusion(bf16[4,2,2,2,2,2,1,128]{7,6,5,4,3,2,1,0:T(2,128)(2,1)S(1)} %copy.38, bf16[4,2,2,2,2,2,1,128]{7,6,5,4,3,2,1,0:T(2,128)(2,1)S(1)} %copy.37, bf16[4,2,2,2,2,2,64,128]{7,6,5,4,3,2,1,0:T(8,128)(2,1)} %bitcast.52), kind=kLoop, calls=%fused_computation | loop fusion | flops 6488064 | bytes 4325376 | tf_op jit(solution)/shard_map/concatenate | solution.py:239
  3.7 0.2 constant_dynamic-slice_fusion.7
  3.9 0.0 copy-start.5
  3.9 0.8 copy.59
  4.8 0.1 collective-permute-start
  4.9 2.7 %collective-permute-done = bf16[4,2,2,2,2,66,128]{6,3,5,2,1,0,4:T(2,128)(2,1)S(1)} collective-permute-done((bf16[4,2,2,2,2,66,128]{6,3,5,2,1,0,4:T(2,128)(2,1)S(1)}, bf16[4,2,2,2,2,66,128]{6,3,5,2,1,0,4:T(2,128)(2,1)S(1)}, u32[]{:S(2)}, u32[]{:S(2)}) %collective-permute-start) | collective-permute-done | bytes 1081376 | tf_op jit(solution)/shard_map/ppermute | solution.py:247
  7.6 1.3 %broadcast_select_fusion = bf16[4,2,2,2,2,66,128]{6,3,5,2,1,0,4:T(2,128)(2,1)S(1)} fusion(bf16[4,2,2,2,2,66,128]{6,3,5,2,1,0,4:T(2,128)(2,1)S(1)} %collective-permute-done, pred[4]{0:T(512)(128)(4,1)S(1)} %get-tuple-element.28, bf16[4,2,2,2,2,1,66,128]{7,6,5,4,3,2,1,0:T(8,128)(2,1)S(1)} %get-tuple-element.13), kind=kLoop, calls=%fused_computation.1 | loop fusion | flops 540672 | bytes 3244036 | tf_op jit(solution)/shard_map/jit(_where)/select_n | solution.py:249
  8.9 0.4 dynamic-slice_bitcast_fusion
  9.3 3.3 %collective-permute-start.1 = (bf16[4,2,2,2,66,128]{5,3,4,2,1,0:T(2,128)(2,1)S(1)}, bf16[4,2,2,2,66,128]{5,3,4,2,1,0:T(2,128)(2,1)S(1)}, u32[]{:S(2)}, u32[]{:S(2)}) collective-permute-start(bf16[4,2,2,2,66,128]{5,3,4,2,1,0:T(2,128)(2,1)S(1)} %dynamic-slice_bitcast_fusion), channel_id=1, source_target_pairs={{0,2},{1,3},{2,0},{3,1},{4,6},{5,7},{6,4},{7,5},{8,10},{9,11},{10,... | collective-permute-start | bytes 1622024 | tf_op jit(solution)/shard_map/ppermute | solution.py:247
  12.6 0.1 reduce_max.12
  12.6 0.1 reduce_min.12
  12.7 0.0 copy-done.2
  12.7 0.1 convolution_convert_fusion
  12.9 12.3 %collective-permute-done.1 = bf16[4,2,2,2,66,128]{5,3,4,2,1,0:T(2,128)(2,1)S(1)} collective-permute-done((bf16[4,2,2,2,66,128]{5,3,4,2,1,0:T(2,128)(2,1)S(1)}, bf16[4,2,2,2,66,128]{5,3,4,2,1,0:T(2,128)(2,1)S(1)}, u32[]{:S(2)}, u32[]{:S(2)}) %collective-permute-start.1) | collective-permute-done | bytes 540704 | tf_op jit(solution)/shard_map/ppermute | solution.py:247
  25.2 0.6 broadcast_select_fusion.1
  25.8 1.1 %constant_dynamic-slice_fusion.5 = (bf16[4,2,2,1,66,128]{5,3,4,2,1,0:T(2,128)(2,1)S(1)}, bf16[4,2,2,1,66,128]{5,3,4,2,1,0:T(2,128)(2,1)S(1)}) fusion(bf16[4,2,2,2,66,128]{5,3,4,2,1,0:T(2,128)(2,1)S(1)} %broadcast_select_fusion.1, s32[]{:T(128)S(6)} %select_n.91, s32[]{:T(128)S(6)} %select_n.92), kind=kLoop, calls=%fused_computation.29 | loop fusion | bytes 1081352 | tf_op jit(solution)/shard_map/jit(dynamic_index_in_dim)/dynamic_slice | solution.py:245
  26.9 0.3 copy.60
  27.2 2.0 %collective-permute-start.2 = (bf16[4,2,2,66,128]{4,2,3,1,0:T(2,128)(2,1)S(1)}, bf16[4,2,2,66,128]{4,2,3,1,0:T(2,128)(2,1)S(1)}, u32[]{:S(2)}, u32[]{:S(2)}) collective-permute-start(bf16[4,2,2,66,128]{4,2,3,1,0:T(2,128)(2,1)S(1)} %bitcast.54), channel_id=1, source_target_pairs={{0,4},{1,5},{2,6},{3,7},{4,0},{5,1},{6,2},{7,3},{8,12},{9,13},{10,... | collective-permute-start | bytes 811016 | tf_op jit(solution)/shard_map/ppermute | solution.py:247
  29.2 0.7 fusion
  29.9 5.3 %collective-permute-done.2 = bf16[4,2,2,66,128]{4,2,3,1,0:T(2,128)(2,1)S(1)} collective-permute-done((bf16[4,2,2,66,128]{4,2,3,1,0:T(2,128)(2,1)S(1)}, bf16[4,2,2,66,128]{4,2,3,1,0:T(2,128)(2,1)S(1)}, u32[]{:S(2)}, u32[]{:S(2)}) %collective-permute-start.2) | collective-permute-done | bytes 270368 | tf_op jit(solution)/shard_map/ppermute | solution.py:247
  35.2 0.4 broadcast_select_fusion.2
  35.6 0.6 constant_dynamic-slice_fusion.3
  36.2 0.0 copy-start.1
  36.2 0.1 copy.61
  36.3 0.0 copy-start.3
  36.3 0.0 copy-start
  36.4 3.4 %collective-permute-start.3 = (bf16[4,2,66,128]{3,1,2,0:T(2,128)(2,1)S(1)}, bf16[4,2,66,128]{3,1,2,0:T(2,128)(2,1)S(1)}, u32[]{:S(2)}, u32[]{:S(2)}) collective-permute-start(bf16[4,2,66,128]{3,1,2,0:T(2,128)(2,1)S(1)} %bitcast.57), channel_id=1, source_target_pairs={{0,8},{1,9},{2,10},{3,11},{4,12},{5,13},{6,14},{7,15},{8,0},{9,1},... | collective-permute-start | bytes 405512 | tf_op jit(solution)/shard_map/ppermute | solution.py:247
  39.7 0.7 dynamic-slice_bitcast_fusion.1
  40.4 0.2 select_reduce_fusion.1
  40.6 4.3 %collective-permute-done.3 = bf16[4,2,66,128]{3,1,2,0:T(2,128)(2,1)S(1)} collective-permute-done((bf16[4,2,66,128]{3,1,2,0:T(2,128)(2,1)S(1)}, bf16[4,2,66,128]{3,1,2,0:T(2,128)(2,1)S(1)}, u32[]{:S(2)}, u32[]{:S(2)}) %collective-permute-start.3) | collective-permute-done | bytes 135200 | tf_op jit(solution)/shard_map/ppermute | solution.py:247
  44.9 0.2 broadcast_select_fusion.3
  45.1 0.3 constant_dynamic-slice_fusion.1
  45.5 6.5 %collective-permute-start.4 = (bf16[4,66,128]{2,1,0:T(8,128)(2,1)S(1)}, bf16[4,66,128]{2,1,0:T(8,128)(2,1)S(1)}, u32[]{:S(2)}, u32[]{:S(2)}) collective-permute-start(bf16[4,66,128]{2,1,0:T(8,128)(2,1)S(1)} %copy.47), channel_id=1, source_target_pairs={{0,16},{1,17},{2,18},{3,19},{4,20},{5,21},{6,22},{7,23},{8,24},{9,... | collective-permute-start | bytes 202760 | tf_op jit(solution)/shard_map/ppermute | solution.py:247
  52.0 0.1 pad_add_fusion.edge_ref
  52.1 2.2 %collective-permute-done.4 = bf16[4,66,128]{2,1,0:T(8,128)(2,1)S(1)} collective-permute-done((bf16[4,66,128]{2,1,0:T(8,128)(2,1)S(1)}, bf16[4,66,128]{2,1,0:T(8,128)(2,1)S(1)}, u32[]{:S(2)}, u32[]{:S(2)}) %collective-permute-start.4) | collective-permute-done | bytes 67616 | tf_op jit(solution)/shard_map/ppermute | solution.py:247
  54.3 0.1 copy_select_fusion.block_ref
  54.4 2.5 %transforms.1 = (bf16[3,64,128]{2,1,0:T(8,128)(2,1)S(1)}, bf16[2,64,128]{2,1,0:T(8,128)(2,1)S(1)}) custom-call(s32[4]{0:T(128)S(1)} %bitcast.51, s32[4]{0:T(128)S(1)} %pad_add_fusion.edge_ref, bf16[4,66,128]{2,1,0:T(8,128)(2,1)S(1)} %copy_select_fusion.block_ref), custom_call_target="tpu_custom_call" | custom-call | tf_op jit(solution)/shard_map/transforms/pallas_call | solution.py:160
  57.0 0.9 %collective-permute-start.5 = (bf16[64,128]{1,0:T(8,128)(2,1)S(1)}, bf16[64,128]{1,0:T(8,128)(2,1)S(1)}, u32[]{:S(2)}, u32[]{:S(2)}) collective-permute-start(bf16[64,128]{1,0:T(8,128)(2,1)S(1)} %get-tuple-element.21), channel_id=1, source_target_pairs={{0,32},{32,0},{64,96},{96,64},{128,160},{160,128},{192,224},{224,1... | collective-permute-start | bytes 49160 | tf_op jit(solution)/shard_map/ppermute | solution.py:289
  57.9 4.0 %collective-permute-start.6 = (bf16[64,128]{1,0:T(8,128)(2,1)S(1)}, bf16[64,128]{1,0:T(8,128)(2,1)S(1)}, u32[]{:S(2)}, u32[]{:S(2)}) collective-permute-start(bf16[64,128]{1,0:T(8,128)(2,1)S(1)} %get-tuple-element.22), channel_id=1, source_target_pairs={{32,64},{96,128},{160,192},{64,32},{128,96},{192,160},{33,65},{97,... | collective-permute-start | bytes 49160 | tf_op jit(solution)/shard_map/ppermute | solution.py:290
  61.9 0.0 collective-permute-done.5
  62.0 3.6 %collective-permute-done.6 = bf16[64,128]{1,0:T(8,128)(2,1)S(1)} collective-permute-done((bf16[64,128]{1,0:T(8,128)(2,1)S(1)}, bf16[64,128]{1,0:T(8,128)(2,1)S(1)}, u32[]{:S(2)}, u32[]{:S(2)}) %collective-permute-start.6) | collective-permute-done | bytes 16416 | tf_op jit(solution)/shard_map/ppermute | solution.py:290
  65.6 0.1 collective-permute-start.7
  65.7 7.7 %collective-permute-start.8 = (bf16[336,128]{1,0:T(8,128)(2,1)S(1)}, bf16[336,128]{1,0:T(8,128)(2,1)S(1)}, u32[]{:S(2)}, u32[]{:S(2)}) collective-permute-start(bf16[336,128]{1,0:T(8,128)(2,1)S(1)} %pad_maximum_fusion.1.own_ref), channel_id=1, source_target_pairs={{1,2},{3,4},{5,6},{7,8},{9,10},{11,12},{13,14},{15,16},{17,18},{19... | collective-permute-start | bytes 258056 | tf_op jit(solution)/shard_map/ppermute | solution.py:296
  73.4 0.0 collective-permute-done.7.side_ref
  73.4 2.2 %collective-permute-done.8.other_ref = bf16[336,128]{1,0:T(8,128)(2,1)S(1)} collective-permute-done((bf16[336,128]{1,0:T(8,128)(2,1)S(1)}, bf16[336,128]{1,0:T(8,128)(2,1)S(1)}, u32[]{:S(2)}, u32[]{:S(2)}) %collective-permute-start.8) | collective-permute-done | bytes 86048 | tf_op jit(solution)/shard_map/ppermute | solution.py:296
  75.6 12.2 %analysis.1 = bf16[69,64,128]{2,1,0:T(8,128)(2,1)} custom-call(bf16[336,128]{1,0:T(8,128)(2,1)S(1)} %pad_maximum_fusion.1.own_ref, bf16[336,128]{1,0:T(8,128)(2,1)S(1)} %collective-permute-done.7.side_ref, bf16[336,128]{1,0:T(8,128)(2,1)S(1)} %collective-permute-done.8.other_ref, bf16[3,16,128]{2,1,0:T(8,128)(2,1)S(1)} %pad_maximum_fusion.2.coef_ref, ...), custom_call_target="tpu_custom_call" | custom-call | tf_op jit(solution)/shard_map/analysis/pallas_call | solution.py:223
  (18 shorter events, 0.2 us)
Async XLA Ops:
  3.9 1.0 %copy-start.5 = (s32[4]{0:T(128)S(1)}, s32[4]{0:T(128)}, u32[]{:S(2)}) copy-start(s32[4]{0:T(128)} %param.15) | copy-start | bytes 52
  4.8 2.8 %collective-permute-start = (bf16[4,2,2,2,2,66,128]{6,3,5,2,1,0,4:T(2,128)(2,1)S(1)}, bf16[4,2,2,2,2,66,128]{6,3,5,2,1,0,4:T(2,128)(2,1)S(1)}, u32[]{:S(2)}, u32[]{:S(2)}) collective-permute-start(bf16[4,2,2,2,2,66,128]{6,3,5,2,1,0,4:T(2,128)(2,1)S(1)} %bitcast.53), channel_id=1, source_target_pairs={{0,1},{1,0},{2,3},{3,2},{4,5},{5,4},{6,7},{7,6},{8,9},{9,8},{10,11... | collective-permute-start | bytes 3244040 | tf_op jit(solution)/shard_map/ppermute | solution.py:247
  7.5 5.0 %copy-start.4 = (s32[2,16,2]{1,2,0:T(2,128)S(1)}, s32[2,16,2]{1,2,0:T(2,128)}, u32[]{:S(2)}) copy-start(s32[2,16,2]{1,2,0:T(2,128)} %param.16) | copy-start | bytes 772
  7.5 5.2 %copy-start.2 = (bf16[32,256]{1,0:T(8,128)(2,1)S(1)}, bf16[32,256]{1,0:T(8,128)(2,1)}, u32[]{:S(2)}) copy-start(bf16[32,256]{1,0:T(8,128)(2,1)} %constant.74.clone) | copy-start | bytes 49156
  9.3 15.9 %collective-permute-start.1 = (bf16[4,2,2,2,66,128]{5,3,4,2,1,0:T(2,128)(2,1)S(1)}, bf16[4,2,2,2,66,128]{5,3,4,2,1,0:T(2,128)(2,1)S(1)}, u32[]{:S(2)}, u32[]{:S(2)}) collective-permute-start(bf16[4,2,2,2,66,128]{5,3,4,2,1,0:T(2,128)(2,1)S(1)} %dynamic-slice_bitcast_fusion), channel_id=1, source_target_pairs={{0,2},{1,3},{2,0},{3,1},{4,6},{5,7},{6,4},{7,5},{8,10},{9,11},{10,... | collective-permute-start | bytes 1622024 | tf_op jit(solution)/shard_map/ppermute | solution.py:247
  27.2 8.0 %collective-permute-start.2 = (bf16[4,2,2,66,128]{4,2,3,1,0:T(2,128)(2,1)S(1)}, bf16[4,2,2,66,128]{4,2,3,1,0:T(2,128)(2,1)S(1)}, u32[]{:S(2)}, u32[]{:S(2)}) collective-permute-start(bf16[4,2,2,66,128]{4,2,3,1,0:T(2,128)(2,1)S(1)} %bitcast.54), channel_id=1, source_target_pairs={{0,4},{1,5},{2,6},{3,7},{4,0},{5,1},{6,2},{7,3},{8,12},{9,13},{10,... | collective-permute-start | bytes 811016 | tf_op jit(solution)/shard_map/ppermute | solution.py:247
  36.2 18.2 %copy-start.1 = (s32[4,1,1]{0,2,1:T(1,128)S(1)}, s32[4,1,1]{0,2,1:T(1,128)}, u32[]{:S(2)}) copy-start(s32[4,1,1]{0,2,1:T(1,128)} %param.14) | copy-start | bytes 52
  36.3 37.1 %copy-start.3 = (bf16[2,2,16,128]{3,2,1,0:T(8,128)(2,1)S(1)}, bf16[2,2,16,128]{3,2,1,0:T(8,128)(2,1)}, u32[]{:S(2)}) copy-start(bf16[2,2,16,128]{3,2,1,0:T(8,128)(2,1)} %constant.76.clone) | copy-start | bytes 49156
  36.3 39.2 %copy-start = (bf16[69,64,1,1,128]{4,1,3,2,0:T(8,128)(2,1)S(1)}, bf16[69,64,1,1,128]{4,1,3,2,0:T(8,128)(2,1)}, u32[]{:S(2)}) copy-start(bf16[69,64,1,1,128]{4,1,3,2,0:T(8,128)(2,1)} %param.10) | copy-start | bytes 3391492
  36.4 8.6 %collective-permute-start.3 = (bf16[4,2,66,128]{3,1,2,0:T(2,128)(2,1)S(1)}, bf16[4,2,66,128]{3,1,2,0:T(2,128)(2,1)S(1)}, u32[]{:S(2)}, u32[]{:S(2)}) collective-permute-start(bf16[4,2,66,128]{3,1,2,0:T(2,128)(2,1)S(1)} %bitcast.57), channel_id=1, source_target_pairs={{0,8},{1,9},{2,10},{3,11},{4,12},{5,13},{6,14},{7,15},{8,0},{9,1},... | collective-permute-start | bytes 405512 | tf_op jit(solution)/shard_map/ppermute | solution.py:247
  45.5 8.8 %collective-permute-start.4 = (bf16[4,66,128]{2,1,0:T(8,128)(2,1)S(1)}, bf16[4,66,128]{2,1,0:T(8,128)(2,1)S(1)}, u32[]{:S(2)}, u32[]{:S(2)}) collective-permute-start(bf16[4,66,128]{2,1,0:T(8,128)(2,1)S(1)} %copy.47), channel_id=1, source_target_pairs={{0,16},{1,17},{2,18},{3,19},{4,20},{5,21},{6,22},{7,23},{8,24},{9,... | collective-permute-start | bytes 202760 | tf_op jit(solution)/shard_map/ppermute | solution.py:247
  57.0 5.0 %collective-permute-start.5 = (bf16[64,128]{1,0:T(8,128)(2,1)S(1)}, bf16[64,128]{1,0:T(8,128)(2,1)S(1)}, u32[]{:S(2)}, u32[]{:S(2)}) collective-permute-start(bf16[64,128]{1,0:T(8,128)(2,1)S(1)} %get-tuple-element.21), channel_id=1, source_target_pairs={{0,32},{32,0},{64,96},{96,64},{128,160},{160,128},{192,224},{224,1... | collective-permute-start | bytes 49160 | tf_op jit(solution)/shard_map/ppermute | solution.py:289
  57.9 7.7 %collective-permute-start.6 = (bf16[64,128]{1,0:T(8,128)(2,1)S(1)}, bf16[64,128]{1,0:T(8,128)(2,1)S(1)}, u32[]{:S(2)}, u32[]{:S(2)}) collective-permute-start(bf16[64,128]{1,0:T(8,128)(2,1)S(1)} %get-tuple-element.22), channel_id=1, source_target_pairs={{32,64},{96,128},{160,192},{64,32},{128,96},{192,160},{33,65},{97,... | collective-permute-start | bytes 49160 | tf_op jit(solution)/shard_map/ppermute | solution.py:290
  65.6 7.8 %collective-permute-start.7 = (bf16[336,128]{1,0:T(8,128)(2,1)S(1)}, bf16[336,128]{1,0:T(8,128)(2,1)S(1)}, u32[]{:S(2)}, u32[]{:S(2)}) collective-permute-start(bf16[336,128]{1,0:T(8,128)(2,1)S(1)} %pad_maximum_fusion.1.own_ref), channel_id=1, source_target_pairs={{0,1},{1,0},{2,3},{3,2},{4,5},{5,4},{6,7},{7,6},{8,9},{9,8},{10,11... | collective-permute-start | bytes 258056 | tf_op jit(solution)/shard_map/ppermute | solution.py:295
  65.7 9.9 %collective-permute-start.8 = (bf16[336,128]{1,0:T(8,128)(2,1)S(1)}, bf16[336,128]{1,0:T(8,128)(2,1)S(1)}, u32[]{:S(2)}, u32[]{:S(2)}) collective-permute-start(bf16[336,128]{1,0:T(8,128)(2,1)S(1)} %pad_maximum_fusion.1.own_ref), channel_id=1, source_target_pairs={{1,2},{3,4},{5,6},{7,8},{9,10},{11,12},{13,14},{15,16},{17,18},{19... | collective-permute-start | bytes 258056 | tf_op jit(solution)/shard_map/ppermute | solution.py:296
